TPU v7x, 256 devices: a whole 4x4x8 slice. The times are simulated.
256 devices in a mesh: hst: 32 (over x_lo, z, core), tp: 8 (over y, x_hi).
Axes of the slice: x: 4 (x_hi: 2, x_lo: 2; x = x_hi * 2 + x_lo), y: 4, z: 8, core: 2. Of those that a mesh axis runs over, the one named last changes fastest.
Arguments:
- queries: bfloat16 [16384, 4096], P('hst', 'tp'), may hold values from -94 to 94
- key_states: bfloat16 [16384, 1024], P('hst', 'tp'), may hold values from -8.5 to 8.5
- value_states: bfloat16 [16384, 1024], P('hst', 'tp'), may hold values from -15 to 15
- passing: int32 [32, 256], P('hst'), may hold values from 0 to 511, as said below
- out_weight: bfloat16 [4096, 7168], P('tp'), may hold values from -0.5 to 0.5
- residual: bfloat16 [16384, 7168], P(('hst', 'tp')), may hold values from -6 to 6
- norm_gain: bfloat16 [7168], replicated, may hold values from 0.5 to 1.5
Outputs:
- stream: bfloat16 [16384, 7168], P(('hst', 'tp'))
- normed: bfloat16 [16384, 7168], P(('hst', 'tp'))
Inputs may be any that keep to these rules, and one draw needn't show every extreme that they name: `passing`: each row lists 256 different positions within its block; the first is 0 and the last is 511.
All inputs are finite; a program needn't handle non-finite values.
Results may differ from a plain program's by a relative error of at most 0.018.
Values may be sent and summed in bfloat16 or wider, within the bound.
A program may use at most 192 MiB of HBM per device.

v0:
```python
import math

import jax
import jax.numpy as jnp
from jax import lax
from jax.sharding import PartitionSpec as P

HEAD = 128


def spread_2(value, axis, source):
    kept = jnp.where(lax.axis_index(axis) == source, value, 0).astype(value.dtype)
    return lax.psum(kept, axis)


def absorb(attn_state, query_heads, key_rows, value_rows, visible):
    row_peaks, totals, running = attn_state
    head_width = query_heads.shape[2]
    factor = 1.0 / math.sqrt(head_width)
    new_peaks = []
    new_totals = []
    new_running = []
    for query_head in range(query_heads.shape[1]):
        scores = (
            jnp.einsum(
                "id,jd->ij",
                query_heads[:, query_head, :],
                key_rows,
                preferred_element_type=jnp.float32,
            )
            * factor
        )
        scores = jnp.where(visible, scores, -jnp.inf)
        newest = jnp.maximum(row_peaks[query_head], jnp.max(scores, axis=1))
        shrink = jnp.exp(row_peaks[query_head] - newest)
        weights = jnp.exp(scores - newest[:, None])
        new_totals.append(totals[query_head] * shrink + jnp.sum(weights, axis=1))
        new_running.append(
            running[query_head] * shrink[:, None]
            + jnp.dot(weights.astype(jnp.bfloat16), value_rows, preferred_element_type=jnp.float32)
        )
        new_peaks.append(newest)
    return (jnp.stack(new_peaks), jnp.stack(new_totals), jnp.stack(new_running))


def on_device(queries, key_states, value_states, passing, out_weight, residual, norm_gain):
    block_index = lax.axis_index("hst")
    row_count = queries.shape[0]
    local_heads = queries.shape[1] // HEAD
    query_heads = queries.reshape(row_count, local_heads, HEAD)
    kv_stack = jnp.stack([key_states, value_states])
    positions = jnp.arange(row_count)
    causal = positions[None, :] <= positions[:, None]
    initial = (
        jnp.full((local_heads, row_count), -jnp.inf, jnp.float32),
        jnp.zeros((local_heads, row_count), jnp.float32),
        jnp.zeros((local_heads, row_count, HEAD), jnp.float32),
    )
    attn_state = absorb(initial, query_heads, key_states, value_states, causal)
    anchor = spread_2(kv_stack, "hst", 0)
    anchor_seen = jnp.full((1, 1), block_index >= 1)
    attn_state = absorb(attn_state, query_heads, anchor[0], anchor[1], anchor_seen)
    retained = kv_stack[:, passing[0], :]
    kept_rows = passing.shape[1]

    def visible_from(first_row, row_total):
        root = (first_row + jnp.arange(row_total)) // kept_rows
        return ((root >= 1) & (root <= block_index - 1))[None, :]

    gathered = lax.all_gather(retained, "hst", axis=1, tiled=True)
    turn_rows = 4 * kept_rows

    def one_turn(turn_number, running_state):
        first_row = turn_number * turn_rows
        kv_piece = lax.dynamic_slice_in_dim(gathered, first_row, turn_rows, 1)
        return absorb(
            running_state, query_heads, kv_piece[0], kv_piece[1], visible_from(first_row, turn_rows)
        )

    attn_state = lax.fori_loop(0, (block_index + 3) // 4, one_turn, attn_state)
    row_peaks, totals, running = attn_state
    attended = (running / totals[:, :, None]).astype(jnp.bfloat16)
    attended = jnp.transpose(attended, (1, 0, 2)).reshape(row_count, local_heads * HEAD)
    partial_sum = jnp.dot(attended, out_weight, preferred_element_type=jnp.float32)
    combined = lax.psum_scatter(
        partial_sum.astype(jnp.bfloat16), "tp", scatter_dimension=0, tiled=True
    ).astype(jnp.float32)
    combined = combined + residual.astype(jnp.float32)
    stream = combined.astype(jnp.bfloat16)
    spread = jnp.mean(combined * combined, axis=1, keepdims=True)
    normed = (combined * lax.rsqrt(spread + 1e-05) * norm_gain.astype(jnp.float32)).astype(
        jnp.bfloat16
    )
    return (stream, normed)


def solution(mesh):
    placed = (
        P("hst", "tp"),
        P("hst", "tp"),
        P("hst", "tp"),
        P("hst", None),
        P("tp", None),
        P(("hst", "tp"), None),
        P(),
    )
    return jax.shard_map(
        on_device,
        mesh=mesh,
        in_specs=placed,
        out_specs=(P(("hst", "tp"), None), P(("hst", "tp"), None)),
        check_vma=False,
    )
```

profile of v0, /device:TPU:3, one launch (start us, length us, event | category | flops | bytes accessed | tf_op | source)
XLA Modules:
  0.0 511.3 jit_solution(13197478930442931644)
XLA Ops:
  7.2 1.2 copy.36
  8.4 1.2 copy.35
  9.6 1.4 broadcast_select_fusion
  11.1 1.6 gather_fusion
  13.6 1.0 copy-done.2
  16.3 217.1 %all-reduce.2.cloned.1.call-done = bf16[2,512,128]{2,0,1:T(2,128)(2,1)} async-done(((bf16[2,512,128]{2,0,1:T(2,128)(2,1)}), bf16[2,512,128]{2,0,1:T(2,128)(2,1)}) %all-reduce.2.cloned.1.call-update) | async-done | bytes 262160 | tf_op jit(solution)/shard_map/psum | solution.py:13
  233.4 1.5 fusion.113
  241.2 60.7 %all-gather.3.cloned.1.call-done = bf16[2,8192,128]{2,0,1:T(2,128)(2,1)} async-done(((bf16[2,256,128]{2,0,1:T(2,128)(2,1)}), bf16[2,8192,128]{2,0,1:T(2,128)(2,1)}) %all-gather.3.cloned.1.call-update) | async-done | bytes 4194320 | tf_op jit(solution)/shard_map/all_gather | solution.py:70
  301.9 51.4 %while.17 = (s32[]{:T(128)}, f32[4,512]{1,0:T(4,128)S(1)}, f32[4,512]{1,0:T(4,128)S(1)}, f32[4,512,128]{2,1,0:T(8,128)S(1)}, s32[]{:T(128)}, /*index=5*/s32[]{:T...) while((s32[]{:T(128)}, f32[4,512]{1,0:T(4,128)S(1)}, ...), condition=%wide.region_26.27_spmd, body=%wide.region_17.26_spmd.sunk | while | flops 1098161152 | bytes 38453456 | solution.py:80
  301.9 2.1 constant_dynamic-slice_fusion.3
  304.0 0.5 fusion.178
  304.5 0.4 fusion.180
  305.0 0.4 fusion.181
  305.4 1.3 fusion.182
  306.7 1.8 fusion.183
  308.6 0.9 fusion.184
  309.4 0.9 fusion.185
  310.3 0.9 fusion.186
  311.2 0.9 fusion.187
  312.2 2.1 constant_dynamic-slice_fusion.3
  314.3 0.5 fusion.178
  314.8 0.4 fusion.180
  315.3 0.4 fusion.181
  315.7 1.3 fusion.182
  317.0 1.8 fusion.183
  318.9 0.9 fusion.184
  319.7 0.9 fusion.185
  320.6 0.9 fusion.186
  321.5 0.9 fusion.187
  322.5 2.1 constant_dynamic-slice_fusion.3
  324.6 0.5 fusion.178
  325.1 0.4 fusion.180
  325.5 0.4 fusion.181
  326.0 1.3 fusion.182
  327.3 1.8 fusion.183
  329.1 0.9 fusion.184
  330.0 0.9 fusion.185
  330.9 0.9 fusion.186
  331.8 0.9 fusion.187
  332.8 2.1 constant_dynamic-slice_fusion.3
  334.9 0.5 fusion.178
  335.4 0.4 fusion.180
  335.9 0.4 fusion.181
  336.3 1.3 fusion.182
  337.6 1.8 fusion.183
  339.5 0.9 fusion.184
  340.3 0.9 fusion.185
  341.2 0.9 fusion.186
  342.1 0.9 fusion.187
  343.1 2.1 constant_dynamic-slice_fusion.3
  345.2 0.5 fusion.178
  345.7 0.4 fusion.180
  346.1 0.4 fusion.181
  346.6 1.3 fusion.182
  347.9 1.8 fusion.183
  349.7 0.9 fusion.184
  350.6 0.9 fusion.185
  351.5 0.9 fusion.186
  352.4 0.9 fusion.187
  353.8 9.2 %convolution_convert_fusion = bf16[512,7168]{1,0:T(8,128)(2,1)} fusion(bf16[512,512]{0,1:T(8,128)(2,1)S(1)} %bitcast.250, bf16[512,7168]{1,0:T(8,128)(2,1)} %param.13), kind=kOutput, calls=%fused_computation.94 | convolution fusion | flops 3761766400 | bytes 15204352 | tf_op jit(solution)/shard_map/dot_general | solution.py:84
  363.0 0.7 copy-done.9
  363.7 137.8 %reduce-scatter.2.cloned.1.call-done = bf16[64,7168]{1,0:T(8,128)(2,1)} async-done(((bf16[512,7168]{1,0:T(8,128)(2,1)}), bf16[64,7168]{1,0:T(8,128)(2,1)}) %reduce-scatter.2.cloned.1.call-update) | async-done | bytes 917520 | tf_op jit(solution)/shard_map/reduce_scatter | solution.py:85
  501.5 1.7 multiply_reduce_fusion
  503.2 1.6 multiply_convert_fusion
  (125 shorter events, 10.7 us)
Async XLA Ops:
  7.2 3.9 copy-start.10
  7.2 5.6 %copy-start.7 = (bf16[512,512]{1,0:T(8,128)(2,1)S(1)}, bf16[512,512]{1,0:T(8,128)(2,1)}, u32[]{:S(2)}) copy-start(bf16[512,512]{1,0:T(8,128)(2,1)} %param.9) | copy-start | bytes 1572868
  7.2 226.2 %all-reduce.2.cloned.1.call-start = ((), (), s32[]{:S(2)}) async-start(), calls=%async_computation.1 | async-start | bytes 524288 | tf_op jit(solution)/shard_map/psum | solution.py:13
  8.4 4.9 copy-start.8
  11.0 290.8 %all-gather.3.cloned.1.call-start = ((), (), s32[]{:S(2)}) async-start(), calls=%async_computation.3 | async-start | bytes 4325376 | tf_op jit(solution)/shard_map/all_gather | solution.py:70
  12.7 488.8 %reduce-scatter.2.cloned.1.call-start = ((), (), s32[]{:S(2)}) async-start(), calls=%async_computation.2 | async-start | bytes 8257536 | tf_op jit(solution)/shard_map/reduce_scatter | solution.py:85
  13.6 1.0 copy-start.2
  15.1 1.0 copy-start
  236.8 1.2 copy-start.3
  236.8 1.2 copy-start.6
  237.6 1.3 copy-start.1
  363.0 0.7 copy-start.9
  363.0 138.5 %copy-start.4 = (bf16[64,7168]{1,0:T(8,128)(2,1)S(1)}, bf16[64,7168]{1,0:T(8,128)(2,1)}, u32[]{:S(2)}) copy-start(bf16[64,7168]{1,0:T(8,128)(2,1)} %param.14) | copy-start | bytes 2752516
  501.5 1.7 copy-start.5
Sparse Core Ops, SparseCore 0:
  11.2 222.1 all-reduce.1
  235.9 65.8 all-gather.2
  363.1 138.3 reduce-scatter.1
where the time goes:
time: 513 us; the launch traced here: 511 us
  waiting for transfers between devices  416 us (81%)
  matrix products  45.2 us (9%)
  local copies, waits for them, and re-layouts  18.8 us (4%)
  other arithmetic  16.8 us (3%)
  between operations  14 us (3%)
    psum x1, waiting for transfers between devices, spread_2(): return lax.psum(kept, axis)  217 us
    reduce_scatter x1, waiting for transfers between devices, on_device(): lax.psum_scatter(partial_sum.astype(jnp.bfloat16), 'tp', scatter_dimensio...  138 us
    all_gather x1, waiting for transfers between devices, on_device(): gathered = lax.all_gather(retained, 'hst', axis=1, tiled=True)  60.7 us
    dot_general x28, matrix products, absorb(): jnp.dot(weights.astype(jnp.bfloat16), value_rows, preferred_element_type=...  20.2 us
    dot_general x28, matrix products, absorb(): jnp.einsum('id,jd->ij', query_heads[:, query_head, :], key_rows, preferre...  15.8 us
    reduce_sum x13, other arithmetic, absorb(): new_totals.append(totals[query_head] * shrink + jnp.sum(weights, axis=1))  10.8 us
    slice x5, local copies, waits for them, and re-layouts, one_turn(): kv_piece[1]  10.3 us
  transfers between devices with their start and end apart: 3, of which 3 were waited for; matrix products, arithmetic and copies ran while one was open for 2% of the time, Pallas kernels for 0%

commit v1 on v0

v1 whole, which is shorter than its diff:
```python
import math

import jax
import jax.numpy as jnp
from jax import lax
from jax.experimental import pallas as pl
from jax.experimental.pallas import tpu as pltpu
from jax.sharding import PartitionSpec as P

f32 = jnp.float32
bf16 = jnp.bfloat16
MESH = pl.DeviceIdType.MESH

HEAD = 128
HEADS = 4
BLK = 512
RET = 256
D = 7168
HALF = D // 2
CC = 512
NCH = HALF // CC
QT = 128
LAST = 31
SCALE = math.log2(math.e) / math.sqrt(HEAD)
ROWS = 256
TILES = HEADS * BLK // ROWS
GKEYS = 4 * RET


def kernel(
    q_ref,
    k_ref,
    v_ref,
    pass_ref,
    w_ref,
    res_ref,
    gain_ref,
    stream_ref,
    normed_ref,
    kvbuf,
    qs,
    acc,
    peak,
    wall,
    abuf,
    ast,
    p0buf,
    prec,
    p1buf,
    xsend,
    xrec,
    ssend,
    srec,
    comb,
    resbuf,
    an_send,
    an_recv,
    x_send,
    x_recv,
    z_send,
    z_recv,
    s_send,
    s_recv,
    wl_sem,
    w_send,
    w_recv,
    a_send,
    a_recv,
    y_send,
    y_recv,
    xh_send,
    xh_recv,
    sb_send,
    sb_recv,
    res_sem,
):
    h = lax.axis_index("hst")
    t = lax.axis_index("tp")
    x = h // 16
    z = (h // 2) % 8
    c = h % 2
    y = t // 2
    e = t % 2
    turn = 1 - 2 * (y % 2)
    pr = (y + turn + 2 * c + 4) % 4
    nb = (y + turn + 2 * (1 - c) + 4) % 4

    def dev(x_, z_, c_, y_, e_):
        return (x_ * 16 + z_ * 2 + c_, y_ * 2 + e_)

    x_dev = dev(1 - x, z, c, y, e)
    up_dev = dev(x, (z + 1) % 8, c, y, e)
    down_dev = dev(x, (z + 7) % 8, c, y, e)
    sib_dev = dev(x, z, 1 - c, y, e)
    pr_dev = dev(x, z, c, pr, e)
    pr_cross = dev(x, z, 1 - c, pr, e)
    nb_dev = dev(x, z, c, nb, e)
    nb_cross = dev(x, z, 1 - c, nb, e)
    e_dev = dev(x, z, c, y, 1 - e)
    e_cross = dev(x, z, 1 - c, y, 1 - e)
    partners = (
        x_dev,
        up_dev,
        down_dev,
        sib_dev,
        pr_dev,
        pr_cross,
        nb_dev,
        nb_cross,
        e_dev,
        e_cross,
    )

    def remote(src, dst, send, recv, device):
        return pltpu.make_async_remote_copy(
            src_ref=src,
            dst_ref=dst,
            send_sem=send,
            recv_sem=recv,
            device_id=device,
            device_id_type=MESH,
        )

    col0 = c * HALF

    def w_cols(j):
        return pl.ds(pl.multiple_of(col0 + j * CC, 128), CC)

    def w_local(j):
        return pltpu.make_async_copy(
            w_ref.at[:, w_cols(j)], wall.at[j, pl.ds(0, BLK), :], wl_sem.at[j]
        )

    def w_remote(j):
        return remote(
            w_ref.at[:, w_cols(j)],
            wall.at[j, pl.ds(BLK, BLK), :],
            w_send.at[j],
            w_recv.at[j],
            pr_dev,
        )

    res_copy = pltpu.make_async_copy(res_ref, resbuf, res_sem)

    barrier = pltpu.get_barrier_semaphore()
    for partner in partners:
        pl.semaphore_signal(barrier, inc=1, device_id=partner, device_id_type=MESH)

    @pl.when(h == 0)
    def _():
        pl.semaphore_signal(barrier, inc=1, device_id=(LAST, t), device_id_type=MESH)

    @pl.when(h == LAST)
    def _():
        pl.semaphore_signal(barrier, inc=1, device_id=(0, t), device_id_type=MESH)

    lane = lax.broadcasted_iota(jnp.int32, (BLK, RET), 1)
    sub = lax.broadcasted_iota(jnp.int32, (BLK, RET), 0)
    chosen = jnp.where(h == 0, lane, jnp.broadcast_to(pass_ref[...], (BLK, RET)))
    onehot = (sub == chosen).astype(bf16)
    both = jnp.concatenate([k_ref[...], v_ref[...]], axis=1)
    kept = lax.dot_general(
        onehot, both, (((0,), (0,)), ((), ())), preferred_element_type=f32
    ).astype(bf16)

    @pl.when(h != LAST)
    def _():
        kvbuf[z, c, x, 0] = kept[:, :HEAD]
        kvbuf[z, c, x, 1] = kept[:, HEAD:]

    extra = jnp.where((h == 0) | (h == LAST), 1, 0)
    pl.semaphore_wait(barrier, len(partners) + extra)

    def anchor(i):
        src = (k_ref, v_ref)[i].at[pl.ds(RET, RET), :]
        return remote(src, kvbuf.at[7, 1, 1, i], an_send.at[i], an_recv.at[i], (LAST, t))

    def anchor_in(i):
        src = (k_ref, v_ref)[i].at[pl.ds(RET, RET), :]
        return remote(src, kvbuf.at[7, 1, 1, i], an_send.at[i], an_recv.at[i], (0, t))

    @pl.when(h == 0)
    def _():
        anchor(0).start()
        anchor(1).start()

    @pl.when(h == LAST)
    def _():
        anchor_in(0).wait_recv()
        anchor_in(1).wait_recv()

    def slot(z_, x_):
        return kvbuf.at[z_, c, x_]

    def x_copy():
        return remote(slot(z, x), slot(z, x), x_send.at[0], x_recv.at[0], x_dev)

    def z_copy(direction, d, z_, x_):
        device = up_dev if direction == 0 else down_dev
        return remote(
            slot(z_, x_),
            slot(z_, x_),
            z_send.at[direction, d, x_],
            z_recv.at[direction, d, x_],
            device,
        )

    def s_copy(g, z_, x_):
        return remote(slot(z_, x_), slot(z_, x_), s_send.at[g, x_], s_recv.at[g, x_], sib_dev)

    def s_wait(g, z_, x_):
        theirs = kvbuf.at[z_, 1 - c, x_]
        remote(theirs, theirs, s_send.at[g, x_], s_recv.at[g, x_], sib_dev).wait_recv()

    x_copy().start()
    z_copy(0, 0, z, x).start()
    z_copy(1, 0, z, x).start()
    s_copy(0, z, x).start()
    for j in range(NCH):
        w_remote(j).start()
    for j in range(NCH):
        w_local(j).start()
    res_copy.start()

    quarters = ((y + 2) % 4, pr, nb, y)
    for r in range(4):
        rows = pl.ds(pl.multiple_of(quarters[r] * QT, QT), QT)
        for head in range(HEADS):
            scaled = q_ref[rows, head * HEAD : (head + 1) * HEAD].astype(f32) * SCALE
            high = scaled.astype(bf16)
            low = (scaled - high.astype(f32)).astype(bf16)
            qs[r, head * QT : (head + 1) * QT, :HEAD] = high
            qs[r, head * QT : (head + 1) * QT, HEAD:] = low

    def logits(tile, keys2):
        r, half = tile // 2, tile % 2
        return lax.dot_general(
            qs[r, half * ROWS : (half + 1) * ROWS, :],
            keys2,
            (((1,), (1,)), ((), ())),
            preferred_element_type=f32,
        )

    own_keys = jnp.concatenate([k_ref[...], k_ref[...]], axis=1)
    own_values = jnp.concatenate([v_ref[...], jnp.ones((BLK, HEAD), bf16)], axis=1)
    key_at = lax.broadcasted_iota(jnp.int32, (ROWS, BLK), 1)
    row_at = lax.broadcasted_iota(jnp.int32, (ROWS, BLK), 0) % QT
    for tile in range(TILES):
        scores = logits(tile, own_keys)
        seen = key_at <= row_at + quarters[tile // 2] * QT
        scores = jnp.where(seen, scores, -jnp.inf)
        newest = jnp.max(scores, axis=1, keepdims=True)
        weights = jnp.exp2(scores - newest).astype(bf16)
        rows = pl.ds(tile * ROWS, ROWS)
        peak[rows, :] = jnp.broadcast_to(newest, (ROWS, HEAD))
        acc[rows, :] = jnp.dot(weights, own_values, preferred_element_type=f32)

    x_copy().wait_recv()
    z_copy(0, 0, z, 1 - x).start()
    z_copy(1, 0, z, 1 - x).start()
    s_copy(0, z, 1 - x).start()

    first_key = k_ref[0:1, :]

    def pass_on(d):
        for direction in range(2):
            z_ = (z + 8 - d) % 8 if direction == 0 else (z + d) % 8
            g = 2 * d - 1 + direction
            for x_ in range(2):
                z_copy(direction, d - 1, z_, x_).wait_recv()
                if x_ == direction:
                    z_copy(direction, d, z_, x_).start()
                else:

                    @pl.when(d < 3)
                    def _():
                        z_copy(direction, d, z_, x_).start()

                s_copy(g, z_, x_).start()

    def one_group(g, carry):
        step = (g + 1) // 2
        z_ = (z + 8 + step * (1 - 2 * (g % 2))) % 8

        @pl.when((g % 2 == 1) & (g < 7))
        def _():
            pass_on(step)

        @pl.when(g == 7)
        def _():
            for x_ in range(2):
                z_copy(x_, 3, z_, x_).wait_recv()
                s_copy(g, z_, x_).start()

        for x_ in range(2):
            s_wait(g, z_, x_)

        lowest = z_ * 2
        used = (h >= 1) & ((lowest < h) | (z_ == 7))

        @pl.when(used)
        def _():
            key_parts, value_parts, unit_parts = [], [], []
            for c_ in range(2):
                for x_ in range(2):
                    number = x_ * 16 + z_ * 2 + c_
                    shown = (number < h) | (number == LAST)
                    key_parts.append(jnp.where(shown, kvbuf[z_, c_, x_, 0], first_key))
                    value_parts.append(
                        jnp.where(shown, kvbuf[z_, c_, x_, 1], jnp.zeros((RET, HEAD), bf16))
                    )
                    unit_parts.append(
                        jnp.where(shown, jnp.ones((RET, HEAD), bf16), jnp.zeros((RET, HEAD), bf16))
                    )
            keys = jnp.concatenate(key_parts, axis=0)
            keys2 = jnp.concatenate([keys, keys], axis=1)
            values2 = jnp.concatenate(
                [jnp.concatenate(value_parts, axis=0), jnp.concatenate(unit_parts, axis=0)], axis=1
            )
            all_scores = [logits(tile, keys2) for tile in range(TILES)]
            for tile in range(TILES):
                scores = all_scores[tile]
                rows = pl.ds(tile * ROWS, ROWS)
                before = peak[rows, :]
                newest = jnp.maximum(before, jnp.max(scores, axis=1, keepdims=True))
                shrink = jnp.exp2(before - newest)
                peak[rows, :] = newest
                weights = jnp.exp2(scores - newest[:, :1]).astype(bf16)
                added = jnp.dot(weights, values2, preferred_element_type=f32)
                old = acc[rows, :]
                acc[rows, :] = (
                    jnp.concatenate([old[:, :HEAD] * shrink, old[:, HEAD:] * shrink], axis=1) + added
                )

        return carry

    lax.fori_loop(0, 8, one_group, 0)

    def attended(r, put):
        for head in range(HEADS):
            rows = pl.ds(r * HEADS * QT + head * QT, QT)
            value = (acc[rows, :HEAD] / acc[rows, HEAD:]).astype(bf16)
            put(head, value)

    def put_ast(r):
        def put(head, value):
            ast[r, :, head * HEAD : (head + 1) * HEAD] = value

        return put

    def put_own(tok):
        def put(head, value):
            abuf[tok, 0, c, :, head * HEAD : (head + 1) * HEAD] = value

        return put

    def a_copy(n, src, tok, source, device):
        return remote(
            src, abuf.at[tok, source, c], a_send.at[n], a_recv.at[tok, source, c], device
        )

    def a_copies():
        return (
            a_copy(0, ast.at[0], 0, 1, pr_dev),
            a_copy(1, ast.at[0], 0, 1, nb_cross),
            a_copy(2, ast.at[1], 1, 1, pr_dev),
            a_copy(3, ast.at[1], 0, 0, sib_dev),
            a_copy(4, abuf.at[0, 0, c], 1, 1, nb_cross),
            a_copy(5, abuf.at[1, 0, c], 1, 0, sib_dev),
        )

    copies = a_copies()
    attended(0, put_ast(0))
    copies[0].start()
    copies[1].start()
    attended(1, put_ast(1))
    copies[3].start()
    copies[2].start()
    attended(2, put_own(0))
    copies[4].start()
    attended(3, put_own(1))
    copies[5].start()

    def a_wait(tok, source, block, device):
        ref = abuf.at[tok, source, block]
        remote(ref, ref, a_send.at[0], a_recv.at[tok, source, block], device).wait_recv()

    def project(tok, j):
        total = None
        for source in range(2):
            rows = abuf[tok, source].reshape(2 * QT, BLK)
            term = jnp.dot(
                rows, wall[j, source * BLK : (source + 1) * BLK, :], preferred_element_type=f32
            )
            total = term if total is None else total + term
        return total

    def y_copy(j):
        return remote(p0buf.at[j], prec.at[j], y_send.at[j], y_recv.at[j], nb_dev)

    a_wait(0, 0, 1 - c, sib_dev)
    a_wait(0, 1, c, pr_dev)
    a_wait(0, 1, 1 - c, pr_cross)

    def send_part(j, carry):
        w_local(j).wait()
        w_remote(j).wait_recv()
        p0buf[j] = project(0, j).astype(bf16)
        y_copy(j).start()
        return carry

    lax.fori_loop(0, NCH, send_part, 0)

    a_wait(1, 0, 1 - c, sib_dev)
    a_wait(1, 1, c, pr_dev)
    a_wait(1, 1, 1 - c, pr_cross)

    def own_part(j, carry):
        p1buf[j] = project(1, j)
        return carry

    lax.fori_loop(0, NCH, own_part, 0)

    mine = pl.multiple_of(e * 64, 64)
    other = pl.multiple_of((1 - e) * 64, 64)

    def xh_copy(block_is_own, j):
        n = 0 if block_is_own else 1
        device = e_dev if block_is_own else e_cross
        return remote(
            xsend.at[n, j], xrec.at[c, j], xh_send.at[n, j], xh_recv.at[c, j], device
        )

    def sb_copy(j):
        return remote(ssend.at[j], srec.at[j], sb_send.at[j], sb_recv.at[j], sib_dev)

    def after_y(j, carry):
        y_copy(j).wait_recv()
        p1buf[j] = p1buf[j] + prec[j].astype(f32)
        own_base = c * QT
        sib_base = (1 - c) * QT
        xsend[0, j] = p1buf[j, pl.ds(pl.multiple_of(own_base + other, 64), 64), :].astype(bf16)
        xh_copy(True, j).start()
        xsend[1, j] = p1buf[j, pl.ds(pl.multiple_of(sib_base + other, 64), 64), :].astype(bf16)
        xh_copy(False, j).start()
        ssend[j] = p1buf[j, pl.ds(pl.multiple_of(sib_base + mine, 64), 64), :].astype(bf16)
        sb_copy(j).start()
        return carry

    lax.fori_loop(0, NCH, after_y, 0)

    res_copy.wait()

    def xh_wait(source_range, j):
        ref = xrec.at[source_range, j]
        remote(ref, ref, xh_send.at[0, j], xh_recv.at[source_range, j], e_dev).wait_recv()

    def finish(j, squares):
        xh_wait(c, j)
        cols = w_cols(j)
        kept_rows = pl.ds(pl.multiple_of(c * QT + mine, 64), 64)
        value = p1buf[j, kept_rows, :] + xrec[c, j].astype(f32) + resbuf[:, cols].astype(f32)
        comb[:, cols] = value
        stream_ref[:, cols] = value.astype(bf16)
        squares = squares + jnp.sum(value * value, axis=1, keepdims=True)
        xh_wait(1 - c, j)
        sb_copy(j).wait_recv()
        cols = pl.ds(pl.multiple_of((1 - c) * HALF + j * CC, 128), CC)
        value = srec[j].astype(f32) + xrec[1 - c, j].astype(f32) + resbuf[:, cols].astype(f32)
        comb[:, cols] = value
        stream_ref[:, cols] = value.astype(bf16)
        return squares + jnp.sum(value * value, axis=1, keepdims=True)

    squares = lax.fori_loop(0, NCH, finish, jnp.zeros((64, 1), f32))
    factor = lax.rsqrt(squares / D + 1e-05)

    def normalise(j, carry):
        cols = pl.ds(pl.multiple_of(j * CC, 128), CC)
        normed_ref[:, cols] = (comb[:, cols] * factor * gain_ref[:, cols].astype(f32)).astype(bf16)
        return carry

    lax.fori_loop(0, 2 * NCH, normalise, 0)

    @pl.when(h == 0)
    def _():
        anchor(0).wait_send()
        anchor(1).wait_send()

    x_copy().wait_send()
    for direction in range(2):
        for d in range(4):
            for x_ in range(2):
                if d < 3 or x_ == direction:
                    z_copy(direction, d, z, x_).wait_send()
    for g in range(8):
        for x_ in range(2):
            s_copy(g, z, x_).wait_send()
    for j in range(NCH):
        w_remote(j).wait_send()
        y_copy(j).wait_send()
        xh_copy(True, j).wait_send()
        xh_copy(False, j).wait_send()
        sb_copy(j).wait_send()
    for copy in a_copies():
        copy.wait_send()


def on_device(queries, key_states, value_states, passing, out_weight, residual, norm_gain):
    vmem = pl.BlockSpec(memory_space=pltpu.VMEM)
    anywhere = pl.BlockSpec(memory_space=pl.ANY)
    dma = pltpu.SemaphoreType.DMA
    out = jax.ShapeDtypeStruct((64, D), bf16)
    return pl.pallas_call(
        kernel,
        out_shape=(out, out),
        in_specs=[vmem, vmem, vmem, vmem, anywhere, anywhere, vmem],
        out_specs=(vmem, vmem),
        scratch_shapes=[
            pltpu.VMEM((8, 2, 2, 2, RET, HEAD), bf16),
            pltpu.VMEM((4, HEADS * QT, 2 * HEAD), bf16),
            pltpu.VMEM((HEADS * BLK, 2 * HEAD), f32),
            pltpu.VMEM((HEADS * BLK, HEAD), f32),
            pltpu.VMEM((NCH, 2 * BLK, CC), bf16),
            pltpu.VMEM((2, 2, 2, QT, BLK), bf16),
            pltpu.VMEM((2, QT, BLK), bf16),
            pltpu.VMEM((NCH, 2 * QT, CC), bf16),
            pltpu.VMEM((NCH, 2 * QT, CC), bf16),
            pltpu.VMEM((NCH, 2 * QT, CC), f32),
            pltpu.VMEM((2, NCH, 64, CC), bf16),
            pltpu.VMEM((2, NCH, 64, CC), bf16),
            pltpu.VMEM((NCH, 64, CC), bf16),
            pltpu.VMEM((NCH, 64, CC), bf16),
            pltpu.VMEM((64, D), f32),
            pltpu.VMEM((64, D), bf16),
            dma((2,)),
            dma((2,)),
            dma((1,)),
            dma((1,)),
            dma((2, 4, 2)),
            dma((2, 4, 2)),
            dma((8, 2)),
            dma((8, 2)),
            dma((NCH,)),
            dma((NCH,)),
            dma((NCH,)),
            dma((6,)),
            dma((2, 2, 2)),
            dma((NCH,)),
            dma((NCH,)),
            dma((2, NCH)),
            dma((2, NCH)),
            dma((NCH,)),
            dma((NCH,)),
            dma,
        ],
        compiler_params=pltpu.CompilerParams(
            collective_id=0, has_side_effects=True, vmem_limit_bytes=58 << 20
        ),
        name="layer",
    )(
        queries,
        key_states,
        value_states,
        passing,
        out_weight,
        residual,
        norm_gain.reshape(1, D),
    )


def solution(mesh):
    placed = (
        P("hst", "tp"),
        P("hst", "tp"),
        P("hst", "tp"),
        P("hst", None),
        P("tp", None),
        P(("hst", "tp"), None),
        P(),
    )
    return jax.shard_map(
        on_device,
        mesh=mesh,
        in_specs=placed,
        out_specs=(P(("hst", "tp"), None), P(("hst", "tp"), None)),
        check_vma=False,
    )
```

time: 513 us -> 94.3 us (0.18)
  the two profiles are of different devices: /device:TPU:3 before, /device:TPU:1 now
where the time goes in v1:
time: 94.3 us; the launch traced here: 94.1 us
  Pallas kernels  87.8 us (93%)
  local copies, waits for them, and re-layouts  5.66 us (6%)
    pallas_call x1, Pallas kernels, on_device(): pl.pallas_call(kernel, out_shape=(out, out), in_specs=[vmem, vmem, vmem,...  87.8 us
    unnamed x2, local copies, waits for them, and re-layouts  4.32 us

profile of v1, /device:TPU:1, one launch (start us, length us, event | category | flops | bytes accessed | tf_op | source)
XLA Modules:
  0.0 94.1 jit_solution(7792393107127090263)
XLA Ops:
  0.6 1.3 %reshape.7.gain_ref = bf16[1,7168]{1,0:T(2,128)(2,1)} reshape(bf16[7168]{0:T(1024)(128)(2,1)} %param.13) | data formatting | bytes 28672 | tf_op jit(solution)/shard_map/reshape | solution.py:567
  2.0 87.8 %layer.1 = (bf16[64,7168]{1,0:T(8,128)(2,1)}, bf16[64,7168]{1,0:T(8,128)(2,1)}) custom-call(bf16[512,512]{1,0:T(8,128)(2,1)} %q_ref.1, bf16[512,128]{1,0:T(8,128)(2,1)} %k_ref.1, bf16[512,128]{1,0:T(8,128)(2,1)} %v_ref.1, s32[1,256]{1,0:T(1,128)} %pass_ref.1, bf16[512,7168]{1,0:T(8,128)(2,1)} %w_ref.1, bf16[64,7168]{1,0:T(8,128)(2,1)} %res_ref.1, ...), custom_call_target="tpu_custom_call" | custom-call | tf_op jit(solution)/shard_map/layer/pallas_call | solution.py:513
  89.8 2.2 %copy.11 = bf16[64,7168]{1,0:T(8,128)(2,1)} copy(bf16[64,7168]{1,0:T(8,128)(2,1)} %get-tuple-element.4) | data formatting | bytes 1835008
  91.9 2.2 %copy.12 = bf16[64,7168]{1,0:T(8,128)(2,1)} copy(bf16[64,7168]{1,0:T(8,128)(2,1)} %get-tuple-element.5) | data formatting | bytes 1835008

commit v2 on v1

--- a/solution.py
+++ b/solution.py
@@ -19,6 +19,7 @@
 HALF = D // 2
 CC = 512
 NCH = HALF // CC
+SHARED = 4
 QT = 128
 LAST = 31
 SCALE = math.log2(math.e) / math.sqrt(HEAD)
@@ -28,15 +29,13 @@
 
 
 def kernel(
-    q_ref,
-    k_ref,
-    v_ref,
+    q_hbm,
+    k_hbm,
+    v_hbm,
     pass_ref,
     w_ref,
     res_ref,
-    gain_ref,
-    stream_ref,
-    normed_ref,
+    comb,
     kvbuf,
     qs,
     acc,
@@ -51,8 +50,11 @@
     xrec,
     ssend,
     srec,
-    comb,
     resbuf,
+    q_ref,
+    k_ref,
+    v_ref,
+    in_sem,
     an_send,
     an_recv,
     x_send,
@@ -64,6 +66,8 @@
     wl_sem,
     w_send,
     w_recv,
+    wf_send,
+    wf_recv,
     a_send,
     a_recv,
     y_send,
@@ -131,7 +135,18 @@
             w_ref.at[:, w_cols(j)], wall.at[j, pl.ds(0, BLK), :], wl_sem.at[j]
         )
 
-    def w_remote(j):
+    def w_half(j):
+        rows = pl.ds(pl.multiple_of(x * RET, RET), RET)
+        there = pl.ds(pl.multiple_of(BLK + x * RET, RET), RET)
+        return remote(
+            w_ref.at[rows, w_cols(j)],
+            wall.at[j, there, :],
+            w_send.at[j],
+            w_recv.at[j],
+            pr_dev,
+        )
+
+    def w_whole(j):
         return remote(
             w_ref.at[:, w_cols(j)],
             wall.at[j, pl.ds(BLK, BLK), :],
@@ -140,7 +155,19 @@
             pr_dev,
         )
 
+    def w_across(j, x_):
+        there = wall.at[j, pl.ds(pl.multiple_of(BLK + x_ * RET, RET), RET), :]
+        return remote(there, there, wf_send.at[j], wf_recv.at[j], x_dev)
+
     res_copy = pltpu.make_async_copy(res_ref, resbuf, res_sem)
+
+    loads = (
+        pltpu.make_async_copy(k_hbm, k_ref, in_sem.at[0]),
+        pltpu.make_async_copy(v_hbm, v_ref, in_sem.at[1]),
+        pltpu.make_async_copy(q_hbm, q_ref, in_sem.at[2]),
+    )
+    for load in loads:
+        load.start()
 
     barrier = pltpu.get_barrier_semaphore()
     for partner in partners:
@@ -154,6 +181,8 @@
     def _():
         pl.semaphore_signal(barrier, inc=1, device_id=(0, t), device_id_type=MESH)
 
+    loads[0].wait()
+    loads[1].wait()
     lane = lax.broadcasted_iota(jnp.int32, (BLK, RET), 1)
     sub = lax.broadcasted_iota(jnp.int32, (BLK, RET), 0)
     chosen = jnp.where(h == 0, lane, jnp.broadcast_to(pass_ref[...], (BLK, RET)))
@@ -205,23 +234,26 @@
             device,
         )
 
-    def s_copy(g, z_, x_):
-        return remote(slot(z_, x_), slot(z_, x_), s_send.at[g, x_], s_recv.at[g, x_], sib_dev)
-
-    def s_wait(g, z_, x_):
+    def s_copy(g, z_, x_, i):
+        return remote(slot(z_, x_), slot(z_, x_), s_send.at[g, i], s_recv.at[g, i], sib_dev)
+
+    def s_wait(g, z_, x_, i):
         theirs = kvbuf.at[z_, 1 - c, x_]
-        remote(theirs, theirs, s_send.at[g, x_], s_recv.at[g, x_], sib_dev).wait_recv()
+        remote(theirs, theirs, s_send.at[g, i], s_recv.at[g, i], sib_dev).wait_recv()
 
     x_copy().start()
     z_copy(0, 0, z, x).start()
     z_copy(1, 0, z, x).start()
-    s_copy(0, z, x).start()
-    for j in range(NCH):
-        w_remote(j).start()
+    s_copy(0, z, x, x).start()
+    for j in range(SHARED):
+        w_half(j).start()
+    for j in range(SHARED, NCH):
+        w_whole(j).start()
     for j in range(NCH):
         w_local(j).start()
     res_copy.start()
 
+    loads[2].wait()
     quarters = ((y + 2) % 4, pr, nb, y)
     for r in range(4):
         rows = pl.ds(pl.multiple_of(quarters[r] * QT, QT), QT)
@@ -258,83 +290,106 @@
     x_copy().wait_recv()
     z_copy(0, 0, z, 1 - x).start()
     z_copy(1, 0, z, 1 - x).start()
-    s_copy(0, z, 1 - x).start()
+    s_copy(0, z, 1 - x, 1 - x).start()
 
     first_key = k_ref[0:1, :]
 
-    def pass_on(d):
-        for direction in range(2):
-            z_ = (z + 8 - d) % 8 if direction == 0 else (z + d) % 8
-            g = 2 * d - 1 + direction
-            for x_ in range(2):
-                z_copy(direction, d - 1, z_, x_).wait_recv()
-                if x_ == direction:
-                    z_copy(direction, d, z_, x_).start()
-                else:
-
-                    @pl.when(d < 3)
-                    def _():
-                        z_copy(direction, d, z_, x_).start()
-
-                s_copy(g, z_, x_).start()
+    def place(g, i):
+        inner = (g >= 1) & (g <= 6)
+        d = (g + 1) // 2
+        turned = (z + 8 - d + 2 * d * i) % 8
+        z_ = jnp.where(inner, turned, (z + jnp.where(g == 7, 4, 0)) % 8)
+        x_ = jnp.where(inner, jnp.where(g % 2 == 1, x, 1 - x), i)
+        return z_, x_
+
+    def pass_on(g):
+        d = (g + 1) // 2
+        for i in range(2):
+            z_, x_ = place(g, i)
+            z_copy(i, d - 1, z_, x_).wait_recv()
+
+            @pl.when((d < 3) | (x_ == i))
+            def _():
+                z_copy(i, d, z_, x_).start()
+
+            s_copy(g, z_, x_, i).start()
+
+    def take_last():
+        for i in range(2):
+            z_, x_ = place(7, i)
+            z_copy(i, 3, z_, x_).wait_recv()
+            s_copy(7, z_, x_, i).start()
+
+    def shown_in(number):
+        return (number < h) | ((number == LAST) & (h >= 1))
+
+    def load_group(g):
+        key_parts, value_parts, unit_parts = [], [], []
+        for i in range(2):
+            z_, x_ = place(g, i)
+            for c_ in range(2):
+                shown = shown_in(x_ * 16 + z_ * 2 + c_)
+                key_parts.append(jnp.where(shown, kvbuf[z_, c_, x_, 0], first_key))
+                value_parts.append(
+                    jnp.where(shown, kvbuf[z_, c_, x_, 1], jnp.zeros((RET, HEAD), bf16))
+                )
+                unit_parts.append(
+                    jnp.where(shown, jnp.ones((RET, HEAD), bf16), jnp.zeros((RET, HEAD), bf16))
+                )
+        keys = jnp.concatenate(key_parts, axis=0)
+        keys2 = jnp.concatenate([keys, keys], axis=1)
+        values2 = jnp.concatenate(
+            [jnp.concatenate(value_parts, axis=0), jnp.concatenate(unit_parts, axis=0)], axis=1
+        )
+        return keys2, values2
+
+    def absorb(tile, scores, values2):
+        rows = pl.ds(tile * ROWS, ROWS)
+        before = peak[rows, :]
+        newest = jnp.maximum(before, jnp.max(scores, axis=1, keepdims=True))
+        shrink = jnp.exp2(before - newest)
+        peak[rows, :] = newest
+        weights = jnp.exp2(scores - newest[:, :1]).astype(bf16)
+        added = jnp.dot(weights, values2, preferred_element_type=f32)
+        old = acc[rows, :]
+        acc[rows, :] = (
+            jnp.concatenate([old[:, :HEAD] * shrink, old[:, HEAD:] * shrink], axis=1) + added
+        )
 
     def one_group(g, carry):
-        step = (g + 1) // 2
-        z_ = (z + 8 + step * (1 - 2 * (g % 2))) % 8
-
-        @pl.when((g % 2 == 1) & (g < 7))
+        @pl.when(g <= 5)
         def _():
-            pass_on(step)
-
-        @pl.when(g == 7)
+            pass_on(g + 1)
+
+        @pl.when(g == 6)
         def _():
-            for x_ in range(2):
-                z_copy(x_, 3, z_, x_).wait_recv()
-                s_copy(g, z_, x_).start()
-
-        for x_ in range(2):
-            s_wait(g, z_, x_)
-
-        lowest = z_ * 2
-        used = (h >= 1) & ((lowest < h) | (z_ == 7))
+            take_last()
+
+        @pl.when((g >= 1) & (g <= SHARED))
+        def _():
+            w_half(g - 1).wait_recv()
+            w_across(g - 1, x).start()
+
+        used = False
+        for i in range(2):
+            z_, x_ = place(g, i)
+            s_wait(g, z_, x_, i)
+            for c_ in range(2):
+                used = used | shown_in(x_ * 16 + z_ * 2 + c_)
 
         @pl.when(used)
         def _():
-            key_parts, value_parts, unit_parts = [], [], []
-            for c_ in range(2):
-                for x_ in range(2):
-                    number = x_ * 16 + z_ * 2 + c_
-                    shown = (number < h) | (number == LAST)
-                    key_parts.append(jnp.where(shown, kvbuf[z_, c_, x_, 0], first_key))
-                    value_parts.append(
-                        jnp.where(shown, kvbuf[z_, c_, x_, 1], jnp.zeros((RET, HEAD), bf16))
-                    )
-                    unit_parts.append(
-                        jnp.where(shown, jnp.ones((RET, HEAD), bf16), jnp.zeros((RET, HEAD), bf16))
-                    )
-            keys = jnp.concatenate(key_parts, axis=0)
-            keys2 = jnp.concatenate([keys, keys], axis=1)
-            values2 = jnp.concatenate(
-                [jnp.concatenate(value_parts, axis=0), jnp.concatenate(unit_parts, axis=0)], axis=1
-            )
+            keys2, values2 = load_group(g)
             all_scores = [logits(tile, keys2) for tile in range(TILES)]
             for tile in range(TILES):
-                scores = all_scores[tile]
-                rows = pl.ds(tile * ROWS, ROWS)
-                before = peak[rows, :]
-                newest = jnp.maximum(before, jnp.max(scores, axis=1, keepdims=True))
-                shrink = jnp.exp2(before - newest)
-                peak[rows, :] = newest
-                weights = jnp.exp2(scores - newest[:, :1]).astype(bf16)
-                added = jnp.dot(weights, values2, preferred_element_type=f32)
-                old = acc[rows, :]
-                acc[rows, :] = (
-                    jnp.concatenate([old[:, :HEAD] * shrink, old[:, HEAD:] * shrink], axis=1) + added
-                )
+                absorb(tile, all_scores[tile], values2)
 
         return carry
 
-    lax.fori_loop(0, 8, one_group, 0)
+    lax.fori_loop(0, 7, one_group, 0)
+    for i in range(2):
+        z_, x_ = place(7, i)
+        s_wait(7, z_, x_, i)
 
     def attended(r, put):
         for head in range(HEADS):
@@ -370,16 +425,16 @@
         )
 
     copies = a_copies()
-    attended(0, put_ast(0))
-    copies[0].start()
-    copies[1].start()
-    attended(1, put_ast(1))
-    copies[3].start()
-    copies[2].start()
-    attended(2, put_own(0))
-    copies[4].start()
-    attended(3, put_own(1))
-    copies[5].start()
+    keys2, values2 = load_group(7)
+    all_scores = [logits(tile, keys2) for tile in range(TILES)]
+    puts = (put_ast(0), put_ast(1), put_own(0), put_own(1))
+    sent = ((0, 1), (3, 2), (4,), (5,))
+    for r in range(4):
+        for tile in (2 * r, 2 * r + 1):
+            absorb(tile, all_scores[tile], values2)
+        attended(r, puts[r])
+        for n in sent[r]:
+            copies[n].start()
 
     def a_wait(tok, source, block, device):
         ref = abuf.at[tok, source, block]
@@ -404,7 +459,15 @@
 
     def send_part(j, carry):
         w_local(j).wait()
-        w_remote(j).wait_recv()
+
+        @pl.when(j < SHARED)
+        def _():
+            w_across(j, 1 - x).wait_recv()
+
+        @pl.when(j >= SHARED)
+        def _():
+            w_whole(j).wait_recv()
+
         p0buf[j] = project(0, j).astype(bf16)
         y_copy(j).start()
         return carry
@@ -455,31 +518,20 @@
         ref = xrec.at[source_range, j]
         remote(ref, ref, xh_send.at[0, j], xh_recv.at[source_range, j], e_dev).wait_recv()
 
-    def finish(j, squares):
+    def finish(j, carry):
         xh_wait(c, j)
         cols = w_cols(j)
         kept_rows = pl.ds(pl.multiple_of(c * QT + mine, 64), 64)
-        value = p1buf[j, kept_rows, :] + xrec[c, j].astype(f32) + resbuf[:, cols].astype(f32)
-        comb[:, cols] = value
-        stream_ref[:, cols] = value.astype(bf16)
-        squares = squares + jnp.sum(value * value, axis=1, keepdims=True)
+        value = p1buf[j, kept_rows, :] + xrec[c, j].astype(f32)
+        comb[:, cols] = value + resbuf[:, cols].astype(f32)
         xh_wait(1 - c, j)
         sb_copy(j).wait_recv()
         cols = pl.ds(pl.multiple_of((1 - c) * HALF + j * CC, 128), CC)
-        value = srec[j].astype(f32) + xrec[1 - c, j].astype(f32) + resbuf[:, cols].astype(f32)
-        comb[:, cols] = value
-        stream_ref[:, cols] = value.astype(bf16)
-        return squares + jnp.sum(value * value, axis=1, keepdims=True)
-
-    squares = lax.fori_loop(0, NCH, finish, jnp.zeros((64, 1), f32))
-    factor = lax.rsqrt(squares / D + 1e-05)
-
-    def normalise(j, carry):
-        cols = pl.ds(pl.multiple_of(j * CC, 128), CC)
-        normed_ref[:, cols] = (comb[:, cols] * factor * gain_ref[:, cols].astype(f32)).astype(bf16)
+        value = srec[j].astype(f32) + xrec[1 - c, j].astype(f32)
+        comb[:, cols] = value + resbuf[:, cols].astype(f32)
         return carry
 
-    lax.fori_loop(0, 2 * NCH, normalise, 0)
+    lax.fori_loop(0, NCH, finish, 0)
 
     @pl.when(h == 0)
     def _():
@@ -494,15 +546,26 @@
                     z_copy(direction, d, z, x_).wait_send()
     for g in range(8):
         for x_ in range(2):
-            s_copy(g, z, x_).wait_send()
+            s_copy(g, z, x_, x_).wait_send()
     for j in range(NCH):
-        w_remote(j).wait_send()
         y_copy(j).wait_send()
         xh_copy(True, j).wait_send()
         xh_copy(False, j).wait_send()
         sb_copy(j).wait_send()
+    for j in range(SHARED):
+        w_half(j).wait_send()
+        w_across(j, x).wait_send()
+    for j in range(SHARED, NCH):
+        w_whole(j).wait_send()
     for copy in a_copies():
         copy.wait_send()
+
+
+def norm_kernel(comb, gain, stream_ref, normed_ref):
+    value = comb[...]
+    stream_ref[...] = value.astype(bf16)
+    factor = lax.rsqrt(jnp.mean(value * value, axis=1, keepdims=True) + 1e-05)
+    normed_ref[...] = (value * factor * gain[...].astype(f32)[None, :]).astype(bf16)
 
 
 def on_device(queries, key_states, value_states, passing, out_weight, residual, norm_gain):
@@ -510,11 +573,11 @@
     anywhere = pl.BlockSpec(memory_space=pl.ANY)
     dma = pltpu.SemaphoreType.DMA
     out = jax.ShapeDtypeStruct((64, D), bf16)
-    return pl.pallas_call(
+    combined = pl.pallas_call(
         kernel,
-        out_shape=(out, out),
-        in_specs=[vmem, vmem, vmem, vmem, anywhere, anywhere, vmem],
-        out_specs=(vmem, vmem),
+        out_shape=jax.ShapeDtypeStruct((64, D), f32),
+        in_specs=[anywhere, anywhere, anywhere, vmem, anywhere, anywhere],
+        out_specs=vmem,
         scratch_shapes=[
             pltpu.VMEM((8, 2, 2, 2, RET, HEAD), bf16),
             pltpu.VMEM((4, HEADS * QT, 2 * HEAD), bf16),
@@ -530,8 +593,11 @@
             pltpu.VMEM((2, NCH, 64, CC), bf16),
             pltpu.VMEM((NCH, 64, CC), bf16),
             pltpu.VMEM((NCH, 64, CC), bf16),
-            pltpu.VMEM((64, D), f32),
             pltpu.VMEM((64, D), bf16),
+            pltpu.VMEM((BLK, HEADS * HEAD), bf16),
+            pltpu.VMEM((BLK, HEAD), bf16),
+            pltpu.VMEM((BLK, HEAD), bf16),
+            dma((3,)),
             dma((2,)),
             dma((2,)),
             dma((1,)),
@@ -543,6 +609,8 @@
             dma((NCH,)),
             dma((NCH,)),
             dma((NCH,)),
+            dma((SHARED,)),
+            dma((SHARED,)),
             dma((6,)),
             dma((2, 2, 2)),
             dma((NCH,)),
@@ -564,8 +632,14 @@
         passing,
         out_weight,
         residual,
-        norm_gain.reshape(1, D),
     )
+    return pl.pallas_call(
+        norm_kernel,
+        out_shape=(out, out),
+        in_specs=[vmem, vmem],
+        out_specs=(vmem, vmem),
+        name="norm",
+    )(combined, norm_gain)
 
 
 def solution(mesh):

time: 94.3 us -> 82.4 us (0.87)
  the two profiles are of different devices: /device:TPU:1 before, /device:TPU:3 now
where the time goes in v2:
time: 82.4 us; the launch traced here: 82.2 us
  Pallas kernels  81.6 us (99%)
    pallas_call x1, Pallas kernels, on_device(): pl.pallas_call(kernel, out_shape=jax.ShapeDtypeStruct((64, D), f32), in_s...  78.5 us
    pallas_call x1, Pallas kernels, on_device(): pl.pallas_call(norm_kernel, out_shape=(out, out), in_specs=[vmem, vmem],...  3.08 us

profile of v2, /device:TPU:3, one launch (start us, length us, event | category | flops | bytes accessed | tf_op | source)
XLA Modules:
  0.0 82.2 jit_solution(16120616639118406488)
XLA Ops:
  0.6 78.5 %layer.1.comb = f32[64,7168]{1,0:T(8,128)} custom-call(bf16[512,512]{1,0:T(8,128)(2,1)} %q_hbm.1, bf16[512,128]{1,0:T(8,128)(2,1)} %k_hbm.1, bf16[512,128]{1,0:T(8,128)(2,1)} %v_hbm.1, s32[1,256]{1,0:T(1,128)} %pass_ref.1, bf16[512,7168]{1,0:T(8,128)(2,1)} %w_ref.1, bf16[64,7168]{1,0:T(8,128)(2,1)} %res_ref.1), custom_call_target="tpu_custom_call" | custom-call | tf_op jit(solution)/shard_map/layer/pallas_call | solution.py:576
  79.2 3.1 %norm.1 = (bf16[64,7168]{1,0:T(8,128)(2,1)}, bf16[64,7168]{1,0:T(8,128)(2,1)}) custom-call(f32[64,7168]{1,0:T(8,128)} %layer.1.comb, bf16[7168]{0:T(1024)(128)(2,1)} %gain.1), custom_call_target="tpu_custom_call" | custom-call | tf_op jit(solution)/shard_map/norm/pallas_call | solution.py:636

commit v3 on v2

--- a/solution.py
+++ b/solution.py
@@ -18,8 +18,12 @@
 D = 7168
 HALF = D // 2
 CC = 512
+BEHIND = 3
 NCH = HALF // CC
 SHARED = 4
+SHARED_COLS = 512
+WHOLE = 2
+WHOLE_COLS = (HALF - SHARED * SHARED_COLS) // WHOLE
 QT = 128
 LAST = 31
 SCALE = math.log2(math.e) / math.sqrt(HEAD)
@@ -130,34 +134,29 @@
     def w_cols(j):
         return pl.ds(pl.multiple_of(col0 + j * CC, 128), CC)
 
-    def w_local(j):
-        return pltpu.make_async_copy(
-            w_ref.at[:, w_cols(j)], wall.at[j, pl.ds(0, BLK), :], wl_sem.at[j]
-        )
-
-    def w_half(j):
-        rows = pl.ds(pl.multiple_of(x * RET, RET), RET)
-        there = pl.ds(pl.multiple_of(BLK + x * RET, RET), RET)
+    w_local = pltpu.make_async_copy(
+        w_ref.at[:, pl.ds(pl.multiple_of(col0, 128), HALF)], wall.at[pl.ds(0, BLK), :], wl_sem
+    )
+
+    def w_unit(u):
+        if u < SHARED:
+            start, width, rows = u * SHARED_COLS, SHARED_COLS, RET
+            first = pl.multiple_of(x * RET, RET)
+        else:
+            start, width, rows = SHARED * SHARED_COLS + (u - SHARED) * WHOLE_COLS, WHOLE_COLS, BLK
+            first = 0
         return remote(
-            w_ref.at[rows, w_cols(j)],
-            wall.at[j, there, :],
-            w_send.at[j],
-            w_recv.at[j],
+            w_ref.at[pl.ds(first, rows), pl.ds(pl.multiple_of(col0 + start, 128), width)],
+            wall.at[pl.ds(BLK + first, rows), pl.ds(start, width)],
+            w_send.at[u],
+            w_recv.at[u],
             pr_dev,
         )
 
-    def w_whole(j):
-        return remote(
-            w_ref.at[:, w_cols(j)],
-            wall.at[j, pl.ds(BLK, BLK), :],
-            w_send.at[j],
-            w_recv.at[j],
-            pr_dev,
-        )
-
-    def w_across(j, x_):
-        there = wall.at[j, pl.ds(pl.multiple_of(BLK + x_ * RET, RET), RET), :]
-        return remote(there, there, wf_send.at[j], wf_recv.at[j], x_dev)
+    def w_across(u, x_):
+        first = pl.multiple_of(BLK + x_ * RET, RET)
+        there = wall.at[pl.ds(first, RET), pl.ds(u * SHARED_COLS, SHARED_COLS)]
+        return remote(there, there, wf_send.at[u], wf_recv.at[u], x_dev)
 
     res_copy = pltpu.make_async_copy(res_ref, resbuf, res_sem)
 
@@ -168,6 +167,8 @@
     )
     for load in loads:
         load.start()
+    w_local.start()
+    res_copy.start()
 
     barrier = pltpu.get_barrier_semaphore()
     for partner in partners:
@@ -197,62 +198,6 @@
         kvbuf[z, c, x, 0] = kept[:, :HEAD]
         kvbuf[z, c, x, 1] = kept[:, HEAD:]
 
-    extra = jnp.where((h == 0) | (h == LAST), 1, 0)
-    pl.semaphore_wait(barrier, len(partners) + extra)
-
-    def anchor(i):
-        src = (k_ref, v_ref)[i].at[pl.ds(RET, RET), :]
-        return remote(src, kvbuf.at[7, 1, 1, i], an_send.at[i], an_recv.at[i], (LAST, t))
-
-    def anchor_in(i):
-        src = (k_ref, v_ref)[i].at[pl.ds(RET, RET), :]
-        return remote(src, kvbuf.at[7, 1, 1, i], an_send.at[i], an_recv.at[i], (0, t))
-
-    @pl.when(h == 0)
-    def _():
-        anchor(0).start()
-        anchor(1).start()
-
-    @pl.when(h == LAST)
-    def _():
-        anchor_in(0).wait_recv()
-        anchor_in(1).wait_recv()
-
-    def slot(z_, x_):
-        return kvbuf.at[z_, c, x_]
-
-    def x_copy():
-        return remote(slot(z, x), slot(z, x), x_send.at[0], x_recv.at[0], x_dev)
-
-    def z_copy(direction, d, z_, x_):
-        device = up_dev if direction == 0 else down_dev
-        return remote(
-            slot(z_, x_),
-            slot(z_, x_),
-            z_send.at[direction, d, x_],
-            z_recv.at[direction, d, x_],
-            device,
-        )
-
-    def s_copy(g, z_, x_, i):
-        return remote(slot(z_, x_), slot(z_, x_), s_send.at[g, i], s_recv.at[g, i], sib_dev)
-
-    def s_wait(g, z_, x_, i):
-        theirs = kvbuf.at[z_, 1 - c, x_]
-        remote(theirs, theirs, s_send.at[g, i], s_recv.at[g, i], sib_dev).wait_recv()
-
-    x_copy().start()
-    z_copy(0, 0, z, x).start()
-    z_copy(1, 0, z, x).start()
-    s_copy(0, z, x, x).start()
-    for j in range(SHARED):
-        w_half(j).start()
-    for j in range(SHARED, NCH):
-        w_whole(j).start()
-    for j in range(NCH):
-        w_local(j).start()
-    res_copy.start()
-
     loads[2].wait()
     quarters = ((y + 2) % 4, pr, nb, y)
     for r in range(4):
@@ -263,6 +208,57 @@
             low = (scaled - high.astype(f32)).astype(bf16)
             qs[r, head * QT : (head + 1) * QT, :HEAD] = high
             qs[r, head * QT : (head + 1) * QT, HEAD:] = low
+
+    extra = jnp.where((h == 0) | (h == LAST), 1, 0)
+    pl.semaphore_wait(barrier, len(partners) + extra)
+
+    def anchor(i):
+        src = (k_ref, v_ref)[i].at[pl.ds(RET, RET), :]
+        return remote(src, kvbuf.at[7, 1, 1, i], an_send.at[i], an_recv.at[i], (LAST, t))
+
+    def anchor_in(i):
+        src = (k_ref, v_ref)[i].at[pl.ds(RET, RET), :]
+        return remote(src, kvbuf.at[7, 1, 1, i], an_send.at[i], an_recv.at[i], (0, t))
+
+    @pl.when(h == 0)
+    def _():
+        anchor(0).start()
+        anchor(1).start()
+
+    @pl.when(h == LAST)
+    def _():
+        anchor_in(0).wait_recv()
+        anchor_in(1).wait_recv()
+
+    def slot(z_, x_):
+        return kvbuf.at[z_, c, x_]
+
+    def x_copy():
+        return remote(slot(z, x), slot(z, x), x_send.at[0], x_recv.at[0], x_dev)
+
+    def z_copy(direction, d, z_, x_):
+        device = up_dev if direction == 0 else down_dev
+        return remote(
+            slot(z_, x_),
+            slot(z_, x_),
+            z_send.at[direction, d, x_],
+            z_recv.at[direction, d, x_],
+            device,
+        )
+
+    def s_copy(g, z_, x_, i):
+        return remote(slot(z_, x_), slot(z_, x_), s_send.at[g, i], s_recv.at[g, i], sib_dev)
+
+    def s_wait(g, z_, x_, i):
+        theirs = kvbuf.at[z_, 1 - c, x_]
+        remote(theirs, theirs, s_send.at[g, i], s_recv.at[g, i], sib_dev).wait_recv()
+
+    x_copy().start()
+    z_copy(0, 0, z, x).start()
+    z_copy(1, 0, z, x).start()
+    s_copy(0, z, x, x).start()
+    for u in range(SHARED + WHOLE):
+        w_unit(u).start()
 
     def logits(tile, keys2):
         r, half = tile // 2, tile % 2
@@ -308,7 +304,7 @@
             z_, x_ = place(g, i)
             z_copy(i, d - 1, z_, x_).wait_recv()
 
-            @pl.when((d < 3) | (x_ == i))
+            @pl.when((d < 3) | (x_ != i))
             def _():
                 z_copy(i, d, z_, x_).start()
 
@@ -317,7 +313,7 @@
     def take_last():
         for i in range(2):
             z_, x_ = place(7, i)
-            z_copy(i, 3, z_, x_).wait_recv()
+            z_copy(1 - i, 3, z_, x_).wait_recv()
             s_copy(7, z_, x_, i).start()
 
     def shown_in(number):
@@ -365,10 +361,12 @@
         def _():
             take_last()
 
-        @pl.when((g >= 1) & (g <= SHARED))
-        def _():
-            w_half(g - 1).wait_recv()
-            w_across(g - 1, x).start()
+        for u in range(SHARED):
+
+            @pl.when(g == u + 1)
+            def _():
+                w_unit(u).wait_recv()
+                w_across(u, x).start()
 
         used = False
         for i in range(2):
@@ -445,7 +443,9 @@
         for source in range(2):
             rows = abuf[tok, source].reshape(2 * QT, BLK)
             term = jnp.dot(
-                rows, wall[j, source * BLK : (source + 1) * BLK, :], preferred_element_type=f32
+                rows,
+                wall[source * BLK : (source + 1) * BLK, pl.ds(pl.multiple_of(j * CC, CC), CC)],
+                preferred_element_type=f32,
             )
             total = term if total is None else total + term
         return total
@@ -458,20 +458,23 @@
     a_wait(0, 1, 1 - c, pr_cross)
 
     def send_part(j, carry):
-        w_local(j).wait()
-
-        @pl.when(j < SHARED)
-        def _():
-            w_across(j, 1 - x).wait_recv()
-
-        @pl.when(j >= SHARED)
-        def _():
-            w_whole(j).wait_recv()
+        for u in range(SHARED):
+
+            @pl.when(j == u * SHARED_COLS // CC)
+            def _():
+                w_across(u, 1 - x).wait_recv()
+
+        for u in range(WHOLE):
+
+            @pl.when(j == (SHARED * SHARED_COLS + u * WHOLE_COLS) // CC)
+            def _():
+                w_unit(SHARED + u).wait_recv()
 
         p0buf[j] = project(0, j).astype(bf16)
         y_copy(j).start()
         return carry
 
+    w_local.wait()
     lax.fori_loop(0, NCH, send_part, 0)
 
     a_wait(1, 0, 1 - c, sib_dev)
@@ -497,41 +500,49 @@
     def sb_copy(j):
         return remote(ssend.at[j], srec.at[j], sb_send.at[j], sb_recv.at[j], sib_dev)
 
-    def after_y(j, carry):
-        y_copy(j).wait_recv()
-        p1buf[j] = p1buf[j] + prec[j].astype(f32)
-        own_base = c * QT
-        sib_base = (1 - c) * QT
-        xsend[0, j] = p1buf[j, pl.ds(pl.multiple_of(own_base + other, 64), 64), :].astype(bf16)
-        xh_copy(True, j).start()
-        xsend[1, j] = p1buf[j, pl.ds(pl.multiple_of(sib_base + other, 64), 64), :].astype(bf16)
-        xh_copy(False, j).start()
-        ssend[j] = p1buf[j, pl.ds(pl.multiple_of(sib_base + mine, 64), 64), :].astype(bf16)
-        sb_copy(j).start()
-        return carry
-
-    lax.fori_loop(0, NCH, after_y, 0)
-
-    res_copy.wait()
-
     def xh_wait(source_range, j):
         ref = xrec.at[source_range, j]
         remote(ref, ref, xh_send.at[0, j], xh_recv.at[source_range, j], e_dev).wait_recv()
 
-    def finish(j, carry):
+    def finish(j):
         xh_wait(c, j)
         cols = w_cols(j)
         kept_rows = pl.ds(pl.multiple_of(c * QT + mine, 64), 64)
         value = p1buf[j, kept_rows, :] + xrec[c, j].astype(f32)
-        comb[:, cols] = value + resbuf[:, cols].astype(f32)
+        comb[:, cols] = (value + resbuf[:, cols].astype(f32)).astype(bf16)
         xh_wait(1 - c, j)
         sb_copy(j).wait_recv()
         cols = pl.ds(pl.multiple_of((1 - c) * HALF + j * CC, 128), CC)
         value = srec[j].astype(f32) + xrec[1 - c, j].astype(f32)
-        comb[:, cols] = value + resbuf[:, cols].astype(f32)
+        comb[:, cols] = (value + resbuf[:, cols].astype(f32)).astype(bf16)
+
+    def after_y(j, carry):
+        y_copy(j).wait_recv()
+
+        def summed(first):
+            rows = pl.ds(pl.multiple_of(first, 64), 64)
+            return p1buf[j, rows, :] + prec[j, rows, :].astype(f32)
+
+        own_base = c * QT
+        sib_base = (1 - c) * QT
+        xsend[0, j] = summed(own_base + other).astype(bf16)
+        xh_copy(True, j).start()
+        xsend[1, j] = summed(sib_base + other).astype(bf16)
+        xh_copy(False, j).start()
+        ssend[j] = summed(sib_base + mine).astype(bf16)
+        sb_copy(j).start()
+        p1buf[j, pl.ds(pl.multiple_of(own_base + mine, 64), 64), :] = summed(own_base + mine)
+
+        @pl.when(j >= BEHIND)
+        def _():
+            finish(j - BEHIND)
+
         return carry
 
-    lax.fori_loop(0, NCH, finish, 0)
+    res_copy.wait()
+    lax.fori_loop(0, NCH, after_y, 0)
+    for j in range(NCH - BEHIND, NCH):
+        finish(j)
 
     @pl.when(h == 0)
     def _():
@@ -542,7 +553,7 @@
     for direction in range(2):
         for d in range(4):
             for x_ in range(2):
-                if d < 3 or x_ == direction:
+                if d < 3 or x_ != direction:
                     z_copy(direction, d, z, x_).wait_send()
     for g in range(8):
         for x_ in range(2):
@@ -552,20 +563,24 @@
         xh_copy(True, j).wait_send()
         xh_copy(False, j).wait_send()
         sb_copy(j).wait_send()
+    for u in range(SHARED + WHOLE):
+        w_unit(u).wait_send()
     for j in range(SHARED):
-        w_half(j).wait_send()
         w_across(j, x).wait_send()
-    for j in range(SHARED, NCH):
-        w_whole(j).wait_send()
     for copy in a_copies():
         copy.wait_send()
 
 
-def norm_kernel(comb, gain, stream_ref, normed_ref):
-    value = comb[...]
-    stream_ref[...] = value.astype(bf16)
+def norm_kernel(comb, gain, stream_ref, normed_ref, normed, sems):
+    keep = pltpu.make_async_copy(comb, stream_ref, sems.at[0])
+    keep.start()
+    value = comb[...].astype(f32)
     factor = lax.rsqrt(jnp.mean(value * value, axis=1, keepdims=True) + 1e-05)
-    normed_ref[...] = (value * factor * gain[...].astype(f32)[None, :]).astype(bf16)
+    normed[...] = (value * factor * gain[...].astype(f32)[None, :]).astype(bf16)
+    give = pltpu.make_async_copy(normed, normed_ref, sems.at[1])
+    give.start()
+    keep.wait()
+    give.wait()
 
 
 def on_device(queries, key_states, value_states, passing, out_weight, residual, norm_gain):
@@ -575,7 +590,7 @@
     out = jax.ShapeDtypeStruct((64, D), bf16)
     combined = pl.pallas_call(
         kernel,
-        out_shape=jax.ShapeDtypeStruct((64, D), f32),
+        out_shape=out,
         in_specs=[anywhere, anywhere, anywhere, vmem, anywhere, anywhere],
         out_specs=vmem,
         scratch_shapes=[
@@ -583,7 +598,7 @@
             pltpu.VMEM((4, HEADS * QT, 2 * HEAD), bf16),
             pltpu.VMEM((HEADS * BLK, 2 * HEAD), f32),
             pltpu.VMEM((HEADS * BLK, HEAD), f32),
-            pltpu.VMEM((NCH, 2 * BLK, CC), bf16),
+            pltpu.VMEM((2 * BLK, HALF), bf16),
             pltpu.VMEM((2, 2, 2, QT, BLK), bf16),
             pltpu.VMEM((2, QT, BLK), bf16),
             pltpu.VMEM((NCH, 2 * QT, CC), bf16),
@@ -606,9 +621,9 @@
             dma((2, 4, 2)),
             dma((8, 2)),
             dma((8, 2)),
-            dma((NCH,)),
-            dma((NCH,)),
-            dma((NCH,)),
+            dma,
+            dma((SHARED + WHOLE,)),
+            dma((SHARED + WHOLE,)),
             dma((SHARED,)),
             dma((SHARED,)),
             dma((6,)),
@@ -637,7 +652,8 @@
         norm_kernel,
         out_shape=(out, out),
         in_specs=[vmem, vmem],
-        out_specs=(vmem, vmem),
+        out_specs=(anywhere, anywhere),
+        scratch_shapes=[pltpu.VMEM((64, D), bf16), dma((2,))],
         name="norm",
     )(combined, norm_gain)
 

time: 82.4 us -> 80.5 us (0.977)
  Pallas kernels: 81.6 us -> 79.7 us
    pallas_call x1, Pallas kernels: 78.5 us -> 77.1 us  [on_device(): pl.pallas_call(kernel, out_shape=out, in_specs=[anywhere, anywhere, anywh...]
where the time goes in v3:
time: 80.5 us; the launch traced here: 80.4 us
  Pallas kernels  79.7 us (99%)
    pallas_call x1, Pallas kernels, on_device(): pl.pallas_call(kernel, out_shape=out, in_specs=[anywhere, anywhere, anywh...  77.1 us
    pallas_call x1, Pallas kernels, on_device(): pl.pallas_call(norm_kernel, out_shape=(out, out), in_specs=[vmem, vmem],...  2.68 us

profile of v3, /device:TPU:3, one launch (start us, length us, event | category | flops | bytes accessed | tf_op | source)
XLA Modules:
  0.0 80.4 jit_solution(8996993024087779350)
XLA Ops:
  0.6 77.1 %layer.1.comb = bf16[64,7168]{1,0:T(8,128)(2,1)} custom-call(bf16[512,512]{1,0:T(8,128)(2,1)} %q_hbm.1, bf16[512,128]{1,0:T(8,128)(2,1)} %k_hbm.1, bf16[512,128]{1,0:T(8,128)(2,1)} %v_hbm.1, s32[1,256]{1,0:T(1,128)} %pass_ref.1, bf16[512,7168]{1,0:T(8,128)(2,1)} %w_ref.1, bf16[64,7168]{1,0:T(8,128)(2,1)} %res_ref.1), custom_call_target="tpu_custom_call" | custom-call | tf_op jit(solution)/shard_map/layer/pallas_call | solution.py:591
  77.7 2.7 %norm.1 = (bf16[64,7168]{1,0:T(8,128)(2,1)}, bf16[64,7168]{1,0:T(8,128)(2,1)}) custom-call(bf16[64,7168]{1,0:T(8,128)(2,1)} %layer.1.comb, bf16[7168]{0:T(1024)(128)(2,1)} %gain.1), custom_call_target="tpu_custom_call" | custom-call | tf_op jit(solution)/shard_map/norm/pallas_call | solution.py:651

commit v4 on v3

--- a/solution.py
+++ b/solution.py
@@ -19,6 +19,8 @@
 HALF = D // 2
 CC = 512
 BEHIND = 3
+LOOK = 4
+PART = 16
 NCH = HALF // CC
 SHARED = 4
 SHARED_COLS = 512
@@ -36,7 +38,7 @@
     q_hbm,
     k_hbm,
     v_hbm,
-    pass_ref,
+    pass_hbm,
     w_ref,
     res_ref,
     comb,
@@ -58,6 +60,7 @@
     q_ref,
     k_ref,
     v_ref,
+    pass_ref,
     in_sem,
     an_send,
     an_recv,
@@ -164,6 +167,7 @@
         pltpu.make_async_copy(k_hbm, k_ref, in_sem.at[0]),
         pltpu.make_async_copy(v_hbm, v_ref, in_sem.at[1]),
         pltpu.make_async_copy(q_hbm, q_ref, in_sem.at[2]),
+        pltpu.make_async_copy(pass_hbm, pass_ref, in_sem.at[3]),
     )
     for load in loads:
         load.start()
@@ -184,6 +188,7 @@
 
     loads[0].wait()
     loads[1].wait()
+    loads[3].wait()
     lane = lax.broadcasted_iota(jnp.int32, (BLK, RET), 1)
     sub = lax.broadcasted_iota(jnp.int32, (BLK, RET), 0)
     chosen = jnp.where(h == 0, lane, jnp.broadcast_to(pass_ref[...], (BLK, RET)))
@@ -273,8 +278,9 @@
     own_values = jnp.concatenate([v_ref[...], jnp.ones((BLK, HEAD), bf16)], axis=1)
     key_at = lax.broadcasted_iota(jnp.int32, (ROWS, BLK), 1)
     row_at = lax.broadcasted_iota(jnp.int32, (ROWS, BLK), 0) % QT
+    own_scores = [logits(tile, own_keys) for tile in range(TILES)]
     for tile in range(TILES):
-        scores = logits(tile, own_keys)
+        scores = own_scores[tile]
         seen = key_at <= row_at + quarters[tile // 2] * QT
         scores = jnp.where(seen, scores, -jnp.inf)
         newest = jnp.max(scores, axis=1, keepdims=True)
@@ -424,7 +430,7 @@
 
     copies = a_copies()
     keys2, values2 = load_group(7)
-    all_scores = [logits(tile, keys2) for tile in range(TILES)]
+    all_scores = [logits(tile, keys2) for tile in range(LOOK)]
     puts = (put_ast(0), put_ast(1), put_own(0), put_own(1))
     sent = ((0, 1), (3, 2), (4,), (5,))
     for r in range(4):
@@ -433,6 +439,8 @@
         attended(r, puts[r])
         for n in sent[r]:
             copies[n].start()
+        for tile in range(LOOK + 2 * r, min(LOOK + 2 * r + 2, TILES)):
+            all_scores.append(logits(tile, keys2))
 
     def a_wait(tok, source, block, device):
         ref = abuf.at[tok, source, block]
@@ -574,13 +582,19 @@
 def norm_kernel(comb, gain, stream_ref, normed_ref, normed, sems):
     keep = pltpu.make_async_copy(comb, stream_ref, sems.at[0])
     keep.start()
-    value = comb[...].astype(f32)
-    factor = lax.rsqrt(jnp.mean(value * value, axis=1, keepdims=True) + 1e-05)
-    normed[...] = (value * factor * gain[...].astype(f32)[None, :]).astype(bf16)
-    give = pltpu.make_async_copy(normed, normed_ref, sems.at[1])
-    give.start()
+    gains = gain[...].astype(f32)[None, :]
+    gives = []
+    for n in range(64 // PART):
+        rows = pl.ds(n * PART, PART)
+        value = comb[rows, :].astype(f32)
+        factor = lax.rsqrt(jnp.mean(value * value, axis=1, keepdims=True) + 1e-05)
+        normed[rows, :] = (value * factor * gains).astype(bf16)
+        give = pltpu.make_async_copy(normed.at[rows], normed_ref.at[rows], sems.at[1 + n])
+        give.start()
+        gives.append(give)
     keep.wait()
-    give.wait()
+    for give in gives:
+        give.wait()
 
 
 def on_device(queries, key_states, value_states, passing, out_weight, residual, norm_gain):
@@ -591,7 +605,7 @@
     combined = pl.pallas_call(
         kernel,
         out_shape=out,
-        in_specs=[anywhere, anywhere, anywhere, vmem, anywhere, anywhere],
+        in_specs=[anywhere] * 6,
         out_specs=vmem,
         scratch_shapes=[
             pltpu.VMEM((8, 2, 2, 2, RET, HEAD), bf16),
@@ -612,7 +626,8 @@
             pltpu.VMEM((BLK, HEADS * HEAD), bf16),
             pltpu.VMEM((BLK, HEAD), bf16),
             pltpu.VMEM((BLK, HEAD), bf16),
-            dma((3,)),
+            pltpu.VMEM((1, RET), jnp.int32),
+            dma((4,)),
             dma((2,)),
             dma((2,)),
             dma((1,)),
@@ -653,7 +668,7 @@
         out_shape=(out, out),
         in_specs=[vmem, vmem],
         out_specs=(anywhere, anywhere),
-        scratch_shapes=[pltpu.VMEM((64, D), bf16), dma((2,))],
+        scratch_shapes=[pltpu.VMEM((64, D), bf16), dma((1 + 64 // PART,))],
         name="norm",
     )(combined, norm_gain)
 

time: 80.5 us -> 79.1 us (0.983)
  Pallas kernels: 79.7 us -> 78.4 us
    pallas_call x1, Pallas kernels: 77.1 us -> 75.9 us  [on_device(): pl.pallas_call(kernel, out_shape=out, in_specs=[anywhere] * 6, out_specs=...]
where the time goes in v4:
time: 79.1 us; the launch traced here: 79 us
  Pallas kernels  78.4 us (99%)
    pallas_call x1, Pallas kernels, on_device(): pl.pallas_call(kernel, out_shape=out, in_specs=[anywhere] * 6, out_specs=...  75.9 us
    pallas_call x1, Pallas kernels, on_device(): pl.pallas_call(norm_kernel, out_shape=(out, out), in_specs=[vmem, vmem],...  2.44 us

profile of v4, /device:TPU:3, one launch (start us, length us, event | category | flops | bytes accessed | tf_op | source)
XLA Modules:
  0.0 79.0 jit_solution(3855612578994233794)
XLA Ops:
  0.6 75.9 %layer.1.comb = bf16[64,7168]{1,0:T(8,128)(2,1)} custom-call(bf16[512,512]{1,0:T(8,128)(2,1)} %q_hbm.1, bf16[512,128]{1,0:T(8,128)(2,1)} %k_hbm.1, bf16[512,128]{1,0:T(8,128)(2,1)} %v_hbm.1, s32[1,256]{1,0:T(1,128)} %pass_hbm.1, bf16[512,7168]{1,0:T(8,128)(2,1)} %w_ref.1, bf16[64,7168]{1,0:T(8,128)(2,1)} %res_ref.1), custom_call_target="tpu_custom_call" | custom-call | tf_op jit(solution)/shard_map/layer/pallas_call | solution.py:605
  76.6 2.4 %norm.1 = (bf16[64,7168]{1,0:T(8,128)(2,1)}, bf16[64,7168]{1,0:T(8,128)(2,1)}) custom-call(bf16[64,7168]{1,0:T(8,128)(2,1)} %layer.1.comb, bf16[7168]{0:T(1024)(128)(2,1)} %gain.1), custom_call_target="tpu_custom_call" | custom-call | tf_op jit(solution)/shard_map/norm/pallas_call | solution.py:666
